TPU v7x, 512 devices: a whole 4x8x8 slice. The times are simulated.
512 devices in a mesh: aa: 8 (over z), ba: 16 (over y, core), col: 4 (over x).
Axes of the slice: x: 4, y: 8, z: 8, core: 2. Of those that a mesh axis runs over, the one named last changes fastest.
Arguments:
- tensor: bfloat16 [512, 512, 512], P('aa', 'ba', 'col'), may hold values from -24 to 24
- factor_b_init: float32 [512, 256], P(('ba', 'aa', 'col')), may hold values from -5.2 to 6.8
- factor_c_init: float32 [512, 256], P(('col', 'aa', 'ba')), may hold values from -5.2 to 6.8
Outputs:
- factor_a: float32 [512, 256], P(('aa', 'ba', 'col'))
- factor_b: float32 [512, 256], P(('ba', 'aa', 'col'))
- factor_c: float32 [512, 256], P(('col', 'aa', 'ba'))
All inputs are finite; a program needn't handle non-finite values.
Results may differ from a plain program's by a relative error of at most 0.007.
The roundings to bfloat16 on the way count: a program that leaves them out, or rounds other values in their place, can miss the bound.
Values may be sent and summed in bfloat16 or wider, within the bound.
No kernel may reach another device: no remote copies, remote signals or barrier semaphores. Data moves between devices by JAX's collectives and lax.ppermute only.
A program may use at most 64 MiB of HBM per device.

v0:
```python
import jax
import jax.numpy as jnp
from jax import lax
from jax.sharding import PartitionSpec as P

EPSILON = 1e-06
HIGHEST = lax.Precision.HIGHEST


def gram_of(rows):
    return jnp.dot(rows.T, rows, precision=HIGHEST, preferred_element_type=jnp.float32)


def solve_rows(products, left_gram, right_gram):
    lower = jnp.linalg.cholesky(left_gram * right_gram)
    return jax.scipy.linalg.cho_solve((lower, True), products.T).T


def column_scale(sum_squares, total_rows):
    return jnp.sqrt(sum_squares / total_rows + EPSILON)


def body(tensor, factor_b_init, factor_c_init):
    blk_i, blk_j, blk_k = tensor.shape
    dim_i = blk_i * lax.axis_size("aa")
    dim_j = blk_j * lax.axis_size("ba")
    dim_k = blk_k * lax.axis_size("col")
    b_block = lax.all_gather(factor_b_init, ("aa", "col"), axis=0, tiled=True)
    gram_b, gram_c = lax.psum((gram_of(factor_b_init), gram_of(factor_c_init)), ("aa", "ba", "col"))
    c_block = lax.all_gather(factor_c_init.astype(jnp.bfloat16), ("aa", "ba"), axis=0, tiled=True)
    inner = jnp.einsum("ijk,kr->ijr", tensor, c_block, preferred_element_type=jnp.float32)
    mttkrp_a = lax.psum_scatter(
        jnp.einsum("ijr,jr->ir", inner, b_block, precision=HIGHEST),
        ("ba", "col"),
        scatter_dimension=0,
        tiled=True,
    )
    raw_a = solve_rows(mttkrp_a, gram_b, gram_c)
    squares_a = lax.psum(jnp.sum(raw_a * raw_a, axis=0), ("aa", "ba", "col"))
    factor_a = raw_a / column_scale(squares_a, dim_i)
    gram_a = lax.psum(gram_of(factor_a), ("aa", "ba", "col"))
    gathered_a = lax.all_gather(factor_a, ("ba", "col"), axis=0, tiled=True)
    inner = jnp.einsum("ijk,kr->ijr", tensor, c_block, preferred_element_type=jnp.float32)
    mttkrp_b = lax.psum_scatter(
        jnp.einsum("ijr,ir->jr", inner, gathered_a, precision=HIGHEST),
        ("aa", "col"),
        scatter_dimension=0,
        tiled=True,
    )
    raw_b = solve_rows(mttkrp_b, gram_a, gram_c)
    squares_b = lax.psum(jnp.sum(raw_b * raw_b, axis=0), ("aa", "ba", "col"))
    factor_b = raw_b / column_scale(squares_b, dim_j)
    gram_b_new = lax.psum(gram_of(factor_b), ("aa", "ba", "col"))
    gathered_b = lax.all_gather(factor_b, ("aa", "col"), axis=0, tiled=True)
    a_low = gathered_a.astype(jnp.bfloat16)
    inner = jnp.einsum("ijk,ir->jkr", tensor, a_low, preferred_element_type=jnp.float32)
    mttkrp_c = lax.psum_scatter(
        jnp.einsum("jkr,jr->kr", inner, gathered_b, precision=HIGHEST),
        ("aa", "ba"),
        scatter_dimension=0,
        tiled=True,
    )
    raw_c = solve_rows(mttkrp_c, gram_a, gram_b_new)
    squares_c = lax.psum(jnp.sum(raw_c * raw_c, axis=0), ("aa", "ba", "col"))
    factor_c = raw_c / column_scale(squares_c, dim_k)
    return (factor_a, factor_b, factor_c)


def solution(mesh):
    return jax.shard_map(
        body,
        mesh=mesh,
        in_specs=(P("aa", "ba", "col"), P(("ba", "aa", "col"), None), P(("col", "aa", "ba"), None)),
        out_specs=(
            P(("aa", "ba", "col"), None),
            P(("ba", "aa", "col"), None),
            P(("col", "aa", "ba"), None),
        ),
        check_vma=False,
    )
```

profile of v0, /device:TPU:1, one launch (start us, length us, event | category | flops | bytes accessed | tf_op | source)
XLA Modules:
  0.0 1870.5 jit_solution(606083459391642555)
XLA Ops:
  7.2 0.7 convert_bitcast_fusion
  8.0 39.8 %all-gather.3 = f32[32,1,256]{2,1,0:T(1,128)S(1)} all-gather(f32[1,1,256]{2,1,0:T(1,128)} %bitcast.276), channel_id=1, replica_groups=mesh['aa'=8,'ba'=16,'col'=4] {'aa','col'}, dimensions={0}, use_global_device_ids=true | all-gather | bytes 33792 | tf_op jit(solution)/shard_map/all_gather | solution.py:28
  47.8 61.0 %all-gather.2 = bf16[128,1,256]{2,1,0:T(2,128)(2,1)S(1)} all-gather(bf16[1,1,256]{2,1,0:T(2,128)(2,1)S(1)} %convert_bitcast_fusion), channel_id=1, replica_groups=mesh['aa'=8,'ba'=16,'col'=4] {'aa','ba'}, dimensions={0}, use_global_device_ids=true | all-gather | bytes 66048 | tf_op jit(solution)/shard_map/all_gather | solution.py:30
  108.8 1.0 multiply_reduce_fusion.2
  109.9 0.8 broadcast_multiply_fusion.2
  110.7 0.8 broadcast_multiply_fusion.3
  111.6 1.3 dynamic-slice.9
  112.9 1.3 dynamic-slice.7
  114.2 169.0 %all-reduce.15.cloned.1.call-done = f32[64,256]{1,0:T(8,128)} async-done(((f32[64,256]{1,0:T(8,128)}), f32[64,256]{1,0:T(8,128)}) %all-reduce.15.cloned.1.call-update) | async-done | bytes 65552
  283.2 1.3 dynamic-slice_bitcast_fusion.2
  284.5 271.2 %all-reduce.19.cloned.1.call-done = (f32[256,256]{0,1:T(8,128)}, f32[256,256]{0,1:T(8,128)}) async-done(((f32[256,256]{0,1:T(8,128)}, f32[256,256]{0,1:T(8,128)}), (f32[256,256]{0,1:T(8,128)}, f32[256,256]{0,1:T(8,128)})) %all-reduce.19.cloned.1.call-update) | async-done | bytes 524304 | tf_op jit(solution)/shard_map/psum | solution.py:29
  555.7 1.1 mul.27
  556.9 11.7 cholesky.172
  568.7 9.8 custom-call.17
  579.0 11.7 cholesky.189
  590.8 0.7 compare_reduce_fusion.4
  593.0 4.4 while.6
  593.2 0.6 fusion.67
  593.8 1.4 bitcast_dynamic-update-slice_fusion.6
  595.3 0.6 fusion.67
  595.9 1.4 bitcast_dynamic-update-slice_fusion.6
  597.3 19.7 %custom-call.18 = f32[2,128,128]{1,2,0:T(8,128)S(1)} custom-call(f32[2,128,128]{2,1,0:T(8,128)S(1)} %get-tuple-element.25), custom_call_target="InvertDiagBlocksLowerTriangular" | custom-call | tf_op jit(solution)/shard_map/jit(_cho_solve)/triangular_solve | solution.py:16
  618.2 97.2 %psum.51 = f32[256]{0:T(256)S(1)} all-reduce(f32[256]{0:T(256)S(1)} %mul.28), channel_id=1, replica_groups=mesh['aa'=8,'ba'=16,'col'=4] {'aa','ba','col'}, use_global_device_ids=true, to_apply=%region_7.0 | all-reduce | flops 256 | bytes 2048 | tf_op jit(solution)/shard_map/psum | solution.py:39
  715.4 0.8 broadcast_multiply_fusion.1
  716.2 65.3 %all-gather.4 = f32[64,1,256]{2,1,0:T(1,128)S(1)} all-gather(f32[1,1,256]{2,1,0:T(1,128)S(1)} %bitcast.263), channel_id=2, replica_groups=mesh['aa'=8,'ba'=16,'col'=4] {'ba','col'}, dimensions={0}, use_global_device_ids=true | all-gather | bytes 66560 | tf_op jit(solution)/shard_map/all_gather | solution.py:42
  781.6 0.3 multiply_reduce_fusion.1
  781.9 112.1 %all-reduce.2 = f32[32,256]{1,0:T(8,128)S(1)} all-reduce(f32[32,256]{1,0:T(8,128)S(1)} %bitcast.261), channel_id=5, replica_groups=mesh['aa'=8,'ba'=16,'col'=4] {'aa','col'}, use_global_device_ids=true, to_apply=%region_9.0.clone | all-reduce | flops 8192 | bytes 65536
  894.0 0.6 dynamic-slice_bitcast_fusion.1
  894.6 150.7 %all-reduce.11.cloned.1.call-done = f32[256,256]{0,1:T(8,128)} async-done(((f32[256,256]{0,1:T(8,128)}), f32[256,256]{0,1:T(8,128)}) %all-reduce.11.cloned.1.call-update) | async-done | bytes 262160 | tf_op jit(solution)/shard_map/psum | solution.py:41
  1045.3 1.0 mul.29
  1046.5 11.7 cholesky.206
  1058.2 0.6 compare_reduce_fusion.3
  1058.9 9.8 custom-call.19
  1069.2 11.7 cholesky.223
  1081.0 0.7 compare_reduce_fusion.2
  1083.0 4.0 while.7
  1083.0 0.6 fusion.68
  1083.6 1.4 bitcast_dynamic-update-slice_fusion.7
  1085.0 0.6 fusion.68
  1085.6 1.4 bitcast_dynamic-update-slice_fusion.7
  1087.0 30.3 %custom-call.20 = f32[2,128,128]{1,2,0:T(8,128)S(1)} custom-call(f32[2,128,128]{2,1,0:T(8,128)S(1)} %get-tuple-element.26), custom_call_target="InvertDiagBlocksLowerTriangular" | custom-call | tf_op jit(solution)/shard_map/jit(_cho_solve)/triangular_solve | solution.py:16
  1118.4 97.1 %psum.53 = f32[256]{0:T(256)S(1)} all-reduce(f32[256]{0:T(256)S(1)} %mul.30), channel_id=1, replica_groups=mesh['aa'=8,'ba'=16,'col'=4] {'aa','ba','col'}, use_global_device_ids=true, to_apply=%region_10.0 | all-reduce | flops 256 | bytes 2048 | tf_op jit(solution)/shard_map/psum | solution.py:51
  1215.5 30.2 %all-gather.5 = f32[32,1,256]{2,1,0:T(1,128)S(1)} all-gather(f32[1,1,256]{2,1,0:T(1,128)S(1)} %bitcast.265), channel_id=3, replica_groups=mesh['aa'=8,'ba'=16,'col'=4] {'aa','col'}, dimensions={0}, use_global_device_ids=true | all-gather | bytes 33792 | tf_op jit(solution)/shard_map/all_gather | solution.py:54
  1245.8 1.5 multiply_reduce_fusion
  1247.3 0.8 copy.38
  1248.1 0.8 broadcast_multiply_fusion
  1249.0 1.3 dynamic-slice.11
  1250.3 186.6 %all-reduce.17.cloned.1.call-done = f32[128,256]{1,0:T(8,128)} async-done(((f32[128,256]{1,0:T(8,128)}), f32[128,256]{1,0:T(8,128)}) %all-reduce.17.cloned.1.call-update) | async-done | bytes 131088
  1437.0 1.4 dynamic-slice_bitcast_fusion
  1438.3 264.9 %all-reduce.13.cloned.1.call-done = f32[256,256]{0,1:T(8,128)} async-done(((f32[256,256]{0,1:T(8,128)}), f32[256,256]{0,1:T(8,128)}) %all-reduce.13.cloned.1.call-update) | async-done | bytes 262160 | tf_op jit(solution)/shard_map/psum | solution.py:53
  1703.3 1.0 mul.31
  1704.5 11.7 cholesky.240
  1716.2 0.7 compare_reduce_fusion.1
  1716.9 9.8 custom-call.21
  1727.2 11.7 cholesky.257
  1739.0 0.6 compare_reduce_fusion
  1740.9 4.3 while.8
  1741.2 0.7 fusion.69
  1741.8 1.3 bitcast_dynamic-update-slice_fusion.8
  1743.2 0.7 fusion.69
  1743.9 1.3 bitcast_dynamic-update-slice_fusion.8
  1745.2 19.7 %custom-call.22 = f32[2,128,128]{1,2,0:T(8,128)S(1)} custom-call(f32[2,128,128]{2,1,0:T(8,128)S(1)} %get-tuple-element.27), custom_call_target="InvertDiagBlocksLowerTriangular" | custom-call | tf_op jit(solution)/shard_map/jit(_cho_solve)/triangular_solve | solution.py:16
  1766.1 97.1 %psum.55 = f32[256]{0:T(256)S(1)} all-reduce(f32[256]{0:T(256)S(1)} %mul.32), channel_id=1, replica_groups=mesh['aa'=8,'ba'=16,'col'=4] {'aa','ba','col'}, use_global_device_ids=true, to_apply=%region_13.16 | all-reduce | flops 256 | bytes 2048 | tf_op jit(solution)/shard_map/psum | solution.py:64
  1863.2 0.6 rsqrt_multiply_fusion
  (91 shorter events, 6.3 us)
Async XLA Ops:
  7.2 101.6 %copy-start = (bf16[64,32,128]{2,1,0:T(8,128)(2,1)S(1)}, bf16[64,32,128]{2,1,0:T(8,128)(2,1)}, u32[]{:S(2)}) copy-start(bf16[64,32,128]{2,1,0:T(8,128)(2,1)} %param.6) | copy-start | bytes 1572868
  7.2 102.7 %copy-start.6 = (f32[1,256]{1,0:T(1,128)S(1)}, f32[1,256]{1,0:T(1,128)}, u32[]{:S(2)}) copy-start(f32[1,256]{1,0:T(1,128)} %param.8) | copy-start | bytes 3076
  7.2 103.5 %copy-start.5 = (f32[1,256]{1,0:T(1,128)S(1)}, f32[1,256]{1,0:T(1,128)}, u32[]{:S(2)}) copy-start(f32[1,256]{1,0:T(1,128)} %param.7) | copy-start | bytes 3076
  7.2 276.0 %all-reduce.15.cloned.1.call-start = ((), (), s32[]{:S(2)}) async-start(), calls=%async_computation.2 | async-start | bytes 131072
  109.8 445.8 %all-reduce.19.cloned.1.call-start = ((), (), s32[]{:S(2)}) async-start(), calls=%async_computation.4 | async-start | bytes 1048576 | tf_op jit(solution)/shard_map/psum | solution.py:29
  111.6 933.8 %all-reduce.11.cloned.1.call-start = ((), (), s32[]{:S(2)}) async-start(), calls=%async_computation | async-start | bytes 524288 | tf_op jit(solution)/shard_map/psum | solution.py:41
  593.0 452.4 %copy-start.1 = (f32[256,256]{0,1:T(8,128)S(1)}, f32[256,256]{0,1:T(8,128)}, u32[]{:S(2)}) copy-start(f32[256,256]{0,1:T(8,128)} %get-tuple-element.53) | copy-start | bytes 786436
  715.4 331.0 %copy-start.3 = (f32[256]{0:T(256)}, f32[256]{0:T(256)S(1)}, u32[]{:S(2)}) copy-start(f32[256]{0:T(256)S(1)} %rsqrt_multiply_fusion.2) | copy-start | bytes 3076
  781.5 655.4 %all-reduce.17.cloned.1.call-start = ((), (), s32[]{:S(2)}) async-start(), calls=%async_computation.3 | async-start | bytes 262144
  1086.9 616.3 %copy-start.2 = (f32[256,256]{0,1:T(8,128)S(1)}, f32[256,256]{0,1:T(8,128)}, u32[]{:S(2)}) copy-start(f32[256,256]{0,1:T(8,128)} %all-reduce.11.cloned.1.call-done) | copy-start | bytes 786436
  1215.5 488.7 %copy-start.4 = (f32[256]{0:T(256)}, f32[256]{0:T(256)S(1)}, u32[]{:S(2)}) copy-start(f32[256]{0:T(256)S(1)} %rsqrt_multiply_fusion.1) | copy-start | bytes 3076
  1248.1 455.2 %all-reduce.13.cloned.1.call-start = ((), (), s32[]{:S(2)}) async-start(), calls=%async_computation.1 | async-start | bytes 524288 | tf_op jit(solution)/shard_map/psum | solution.py:53
Sparse Core Ops, SparseCore 0:
  110.0 173.1 all-reduce.14
  288.4 267.2 all-reduce.18
  781.7 263.6 all-reduce.10
  1248.2 188.6 all-reduce.16
  1441.8 261.4 all-reduce.12
where the time goes:
time: 1870 us
  waiting for transfers between devices  1040 us (56%)
  blocking collectives  600 us (32%)
  other arithmetic  181 us (10%)
  local copies, waits for them, and re-layouts  20.6 us (1%)
    unnamed x7, waiting for transfers between devices  356 us
    psum x1, waiting for transfers between devices, body(): lax.psum((gram_of(factor_b_init), gram_of(factor_c_init)), ('aa', 'ba', '...  271 us
    psum x1, waiting for transfers between devices, body(): gram_b_new = lax.psum(gram_of(factor_b), ('aa', 'ba', 'col'))  265 us
    psum x1, waiting for transfers between devices, body(): gram_a = lax.psum(gram_of(factor_a), ('aa', 'ba', 'col'))  151 us
    unnamed x1, blocking collectives  112 us
    another operation x20, other arithmetic, solve_rows(): lower = jnp.linalg.cholesky(left_gram * right_gram)  103 us
    psum x1, blocking collectives, body(): squares_a = lax.psum(jnp.sum(raw_a * raw_a, axis=0), ('aa', 'ba', 'col'))  97.2 us
    psum x1, blocking collectives, body(): squares_c = lax.psum(jnp.sum(raw_c * raw_c, axis=0), ('aa', 'ba', 'col'))  97.1 us
  transfers between devices with their start and end apart: 5, of which 5 were waited for; matrix products, arithmetic and copies ran while one was open for 1% of the time, Pallas kernels for 0%

commit v1 on v0

v1 whole, which is shorter than its diff:
```python
import jax
import jax.numpy as jnp
from jax import lax
from jax.sharding import Mesh, PartitionSpec as P

EPSILON = 1e-06
HIGHEST = lax.Precision.HIGHEST
F32 = jnp.float32


def dot(left, right):
    return jnp.dot(left, right, precision=HIGHEST, preferred_element_type=F32)


def gram_of(rows):
    return lax.dot_general(rows, rows, (((0,), (0,)), ((), ())), precision=HIGHEST, preferred_element_type=F32)


def spd_inverse(matrix):
    lower = jnp.linalg.cholesky(matrix)
    return jax.scipy.linalg.cho_solve((lower, True), jnp.eye(matrix.shape[0], dtype=F32))


def axes_size(axes):
    size = 1
    for axis in axes:
        size *= lax.axis_size(axis)
    return size


def gather(rows, axes):
    size = axes_size(axes)
    copies = jnp.broadcast_to(rows[None], (size,) + rows.shape)
    out = lax.all_to_all(copies, axes, 0, 0, tiled=True)
    return out.reshape((size * rows.shape[0],) + rows.shape[1:])


def reduce_scatter(partial, axes):
    size = axes_size(axes)
    parts = partial.reshape((size, partial.shape[0] // size) + partial.shape[1:])
    return jnp.sum(lax.all_to_all(parts, axes, 0, 0, tiled=True), axis=0)


def normalized(gram, total_rows):
    squares = jnp.sum(jnp.where(jnp.eye(gram.shape[0], dtype=bool), gram, 0.0), axis=0)
    inv_scale = 1.0 / jnp.sqrt(squares / total_rows + EPSILON)
    return inv_scale, gram * inv_scale[:, None] * inv_scale[None, :]


def body(tensor, b_row, c_row):
    blk_i, blk_j, blk_k = tensor.shape
    rank = b_row.shape[1]
    n_aa, n_y, n_core, n_col = (lax.axis_size(axis) for axis in ("aa", "y", "core", "col"))
    dim_i, dim_j, dim_k = blk_i * n_aa, blk_j * n_y * n_core, blk_k * n_col
    y, core, col = lax.axis_index("y"), lax.axis_index("core"), lax.axis_index("col")

    own = gather(jnp.concatenate([b_row, c_row], axis=1), ("aa", "y", "col"))
    other = lax.ppermute(own, "core", [(0, 1), (1, 0)])
    both = jnp.stack([jnp.where(core == 0, own, other), jnp.where(core == 0, other, own)])
    b_block = lax.dynamic_index_in_dim(
        own[:, :rank].reshape(n_aa, n_y, n_col, rank), y, 1, keepdims=False
    ).reshape(blk_j, rank)
    c_block = lax.dynamic_index_in_dim(
        both[:, :, rank:].astype(jnp.bfloat16).reshape(n_core, n_aa, n_y, n_col, rank), col, 3, keepdims=False
    )
    c_block = c_block.transpose(1, 2, 0, 3).reshape(blk_k, rank)
    gram_b = gram_of(both[:, :, :rank].reshape(dim_j, rank))
    gram_c = gram_of(both[:, :, rank:].reshape(dim_k, rank))

    inner = jnp.einsum("ijk,kr->ijr", tensor, c_block, preferred_element_type=F32)
    mttkrp_a = reduce_scatter(jnp.sum(inner * b_block[None], axis=1), ("y", "core", "col"))
    inverse = spd_inverse(gram_b * gram_c)
    raw_a = dot(gather(mttkrp_a, ("y", "core", "col")), inverse)
    all_a = gather(raw_a, ("aa",))

    mttkrp_b = reduce_scatter(jnp.sum(inner * raw_a[:, None], axis=0), ("aa", "col"))
    inv_scale_a, gram_a = normalized(gram_of(all_a), dim_i)
    factor_a = raw_a * inv_scale_a
    inverse = spd_inverse(gram_a * gram_c)
    raw_b = dot(gather(mttkrp_b, ("aa", "col")) * inv_scale_a, inverse)
    all_b = gather(raw_b, ("y", "core"))

    inner = jnp.einsum("ijk,ir->jkr", tensor, factor_a.astype(jnp.bfloat16), preferred_element_type=F32)
    mttkrp_c = reduce_scatter(jnp.sum(inner * raw_b[:, None], axis=0), ("aa", "y", "core"))
    inv_scale_b, gram_b_new = normalized(gram_of(all_b), dim_j)
    factor_b = raw_b * inv_scale_b
    inverse = spd_inverse(gram_a * gram_b_new)
    raw_c = dot(mttkrp_c * inv_scale_b, inverse)
    squares = jnp.sum(gather(raw_c * raw_c, ("y", "core", "col")), axis=0, keepdims=True)
    squares = jnp.sum(gather(squares, ("aa",)), axis=0, keepdims=True)
    factor_c = raw_c / jnp.sqrt(squares / dim_k + EPSILON)

    a_index = (y * n_core + core) * n_col + col
    b_index = lax.axis_index("aa") * n_col + col
    return (
        lax.dynamic_slice_in_dim(factor_a, a_index, 1, 0),
        lax.dynamic_slice_in_dim(factor_b, b_index, 1, 0),
        factor_c,
    )


def solution(mesh):
    n_aa, n_ba, n_col = mesh.devices.shape
    fine = Mesh(mesh.devices.reshape(n_aa, n_ba // 2, 2, n_col), ("aa", "y", "core", "col"))
    a_spec = P(("aa", "y", "core", "col"), None)
    b_spec = P(("y", "core", "aa", "col"), None)
    c_spec = P(("col", "aa", "y", "core"), None)
    return jax.shard_map(
        body,
        mesh=fine,
        in_specs=(P("aa", ("y", "core"), "col"), b_spec, c_spec),
        out_specs=(a_spec, b_spec, c_spec),
        check_vma=False,
    )
```

time: 1870 us -> 393 us (0.21)
  waiting for transfers between devices: 1040 us -> 62.7 us
  blocking collectives: 600 us -> 78.1 us
  starting transfers between devices: 0.21 us -> 36.9 us
    psum x3 -> x0, waiting for transfers between devices: 687 us -> none  [the longest x1 271 us: body(): lax.psum((gram_of(factor_b_init), gram_of(factor_c_init)), ('aa', 'ba', '...]
    unnamed x7 -> x0, waiting for transfers between devices: 356 us -> none
    psum x3 -> x0, blocking collectives: 291 us -> none  [the longest x1 97.2 us: body(): squares_a = lax.psum(jnp.sum(raw_a * raw_a, axis=0), ('aa', 'ba', 'col'))]
    all_gather x4 -> x0, blocking collectives: 196 us -> none  [the longest x1 65.3 us: body(): gathered_a = lax.all_gather(factor_a, ('ba', 'col'), axis=0, tiled=True)]
    unnamed x1 -> x0, blocking collectives: 112 us -> none
    all_to_all x0 -> x3, blocking collectives: none -> 78.1 us  [the longest x1 40.5 us: gather(): out = lax.all_to_all(copies, axes, 0, 0, tiled=True)]
    all_to_all x0 -> x7, waiting for transfers between devices: none -> 62.2 us  [the longest x6 54.9 us: gather(): out = lax.all_to_all(copies, axes, 0, 0, tiled=True)]
    all_to_all x0 -> x7, starting transfers between devices: none -> 31.6 us  [the longest x6 25.9 us: gather(): out = lax.all_to_all(copies, axes, 0, 0, tiled=True)]
  transfers between devices with their start and end apart: 5 -> 8, of which waited for: 5 -> 7; matrix products, arithmetic and copies ran while one was open for 1% -> 17% of each run, Pallas kernels for 0% -> 0%
where the time goes in v1:
time: 393 us; the launch traced here: 388 us
  other arithmetic  167 us (42%)
  blocking collectives  78.1 us (20%)
  waiting for transfers between devices  62.7 us (16%)
  starting transfers between devices  36.9 us (9%)
  local copies, waits for them, and re-layouts  20.7 us (5%)
  matrix products  16.8 us (4%)
  between operations  5.71 us (1%)
    another operation x20, other arithmetic, spd_inverse(): lower = jnp.linalg.cholesky(matrix)  103 us
    another operation x7, other arithmetic, spd_inverse(): jax.scipy.linalg.cho_solve((lower, True), jnp.eye(matrix.shape[0], dtype=...  59.6 us
    all_to_all x6, waiting for transfers between devices, gather(): out = lax.all_to_all(copies, axes, 0, 0, tiled=True)  54.9 us
    all_to_all x1, blocking collectives, gather(): out = lax.all_to_all(copies, axes, 0, 0, tiled=True)  40.5 us
    all_to_all x2, blocking collectives, reduce_scatter(): return jnp.sum(lax.all_to_all(parts, axes, 0, 0, tiled=True), axis=0)  37.5 us
    all_to_all x6, starting transfers between devices, gather(): out = lax.all_to_all(copies, axes, 0, 0, tiled=True)  25.9 us
    another operation x22, local copies, waits for them, and re-layouts, spd_inverse(): jax.scipy.linalg.cho_solve((lower, True), jnp.eye(matrix.shape[0], dtype=...  12 us
  transfers between devices with their start and end apart: 8, of which 7 were waited for; matrix products, arithmetic and copies ran while one was open for 17% of the time, Pallas kernels for 0%

profile of v1, /device:TPU:1, one launch (start us, length us, event | category | flops | bytes accessed | tf_op | source)
XLA Modules:
  0.0 388.1 jit_solution(9309902689265847586)
XLA Ops:
  0.6 0.8 pad_maximum_fusion.2
  1.7 40.5 %all_to_all.50 = f32[256,1,512]{2,1,0:T(1,128)S(1)} all-to-all(f32[256,1,512]{2,1,0:T(1,128)S(1)} %broadcast_in_dim.23), channel_id=1, replica_groups=mesh['aa'=8,'y'=8,'core'=2,'col'=4] {'aa','y','col'}, dimensions={0} | all-to-all | bytes 1048576 | tf_op jit(solution)/shard_map/all_to_all | solution.py:34
  42.3 5.3 %collective-permute-start = (f32[256,512]{1,0:T(8,128)S(1)}, f32[256,512]{1,0:T(8,128)S(1)}, u32[]{:S(2)}, u32[]{:S(2)}) collective-permute-start(f32[256,512]{1,0:T(8,128)S(1)} %bitcast.167), channel_id=1, source_target_pairs={{0,4},{4,0},{1,5},{5,1},{2,6},{6,2},{3,7},{7,3},{8,12},{12,8},{9,1... | collective-permute-start | bytes 1572872 | tf_op jit(solution)/shard_map/ppermute | solution.py:58
  47.8 0.6 mul.110
  49.0 1.0 convolution_bitcast_fusion.2
  50.1 1.0 fusion.3
  51.3 11.7 %cholesky.172 = f32[128,128]{1,0:T(8,128)S(1)} custom-call(f32[128,128]{1,0:T(8,128)S(1)} %cholesky.270), custom_call_target="Cholesky" | custom-call | tf_op jit(solution)/shard_map/jit(cholesky)/cholesky | solution.py:20
  63.0 9.8 %custom-call.17 = f32[1,128,128]{1,2,0:T(8,128)S(1)} custom-call(f32[1,128,128]{2,1,0:T(8,128)S(1)} %get-tuple-element.71), custom_call_target="InvertDiagBlocksLowerTriangular" | custom-call | tf_op jit(solution)/shard_map/jit(cholesky)/cholesky | solution.py:20
  73.3 12.1 %cholesky.189 = f32[128,128]{1,0:T(8,128)S(1)} custom-call(f32[128,128]{1,0:T(8,128)S(1)} %convolution_subtract_fusion.8), custom_call_target="Cholesky" | custom-call | tf_op jit(solution)/shard_map/jit(cholesky)/cholesky | solution.py:20
  85.5 0.6 compare_reduce_fusion.4
  87.5 4.0 %while.6 = (s32[]{:T(128)}, f32[256,256]{1,0:T(8,128)S(1)}, s32[2,2]{1,0:T(2,128)S(1)}, f32[2,128,128]{2,1,0:T(8,128)S(1)}, s32[]{:T(128)}) while((s32[]{:T(128)}, f32[256,256]{1,0:T(8,128)S(1)}, s32[2,2]{1,0:T(2,128)S(1)}, f32[2,128,128]{2,1,0:T(8,128)S(1)}, s32[]{:T(128)}) %tuple.69), condition=%wide.while_cond, body=%wide.while_body.sunk | while | flops 2 | bytes 131181 | solution.py:21
  87.6 0.6 fusion.104
  88.1 1.4 bitcast_dynamic-update-slice_fusion.6
  90.1 1.4 bitcast_dynamic-update-slice_fusion.6
  91.5 19.7 %custom-call.18 = f32[2,128,128]{1,2,0:T(8,128)S(1)} custom-call(f32[2,128,128]{2,1,0:T(8,128)S(1)} %get-tuple-element.25), custom_call_target="InvertDiagBlocksLowerTriangular" | custom-call | tf_op jit(solution)/shard_map/jit(_cho_solve)/triangular_solve | solution.py:21
  113.1 0.6 reshape.151
  113.8 1.4 fusion.1
  115.1 0.7 reshape.121
  115.8 5.7 %all-to-all-start.1 = ((f32[64,1,256]{2,1,0:T(1,128)}), f32[64,1,256]{2,1,0:T(1,128)}, u32[]{:S(2)}, u32[]{:S(2)}) async-start(f32[64,1,256]{2,1,0:T(1,128)} %reshape.121), calls=%async_computation.1 | async-start | bytes 131072 | tf_op jit(solution)/shard_map/all_to_all | solution.py:41
  121.5 1.9 convolution_subtract_fusion.4
  123.4 7.3 %all-to-all-done.1 = f32[64,1,256]{2,1,0:T(1,128)} async-done(((f32[64,1,256]{2,1,0:T(1,128)}), f32[64,1,256]{2,1,0:T(1,128)}, u32[]{:S(2)}, u32[]{:S(2)}) %all-to-all-start.1) | async-done | bytes 65568 | tf_op jit(solution)/shard_map/all_to_all | solution.py:41
  130.7 0.9 reduce_sum.91
  131.6 0.7 broadcast_in_dim.24
  132.3 5.3 %all-to-all-start.2 = ((f32[64,1,256]{2,1,0:T(1,128)}), f32[64,1,256]{2,1,0:T(1,128)S(1)}, u32[]{:S(2)}, u32[]{:S(2)}) async-start(f32[64,1,256]{2,1,0:T(1,128)} %broadcast_in_dim.24), calls=%async_computation.2 | async-start | bytes 131072 | tf_op jit(solution)/shard_map/all_to_all | solution.py:34
  137.6 1.2 fusion.43
  138.8 8.2 %all-to-all-done.2 = f32[64,1,256]{2,1,0:T(1,128)S(1)} async-done(((f32[64,1,256]{2,1,0:T(1,128)}), f32[64,1,256]{2,1,0:T(1,128)S(1)}, u32[]{:S(2)}, u32[]{:S(2)}) %all-to-all-start.2) | async-done | bytes 65568 | tf_op jit(solution)/shard_map/all_to_all | solution.py:34
  147.5 12.8 %all_to_all.51 = f32[32,1,256]{2,1,0:T(1,128)S(1)} all-to-all(f32[32,1,256]{2,1,0:T(1,128)S(1)} %reshape.123), channel_id=1, replica_groups=mesh['aa'=8,'y'=8,'core'=2,'col'=4] {'aa','col'}, dimensions={0} | all-to-all | bytes 65536 | tf_op jit(solution)/shard_map/all_to_all | solution.py:41
  160.3 0.8 broadcast_in_dim.25
  161.2 3.5 all-to-all-start.3
  164.7 14.9 %all-to-all-done.3 = f32[8,64,256]{2,1,0:T(8,128)S(1)} async-done(((f32[8,64,256]{2,1,0:T(8,128)}), f32[8,64,256]{2,1,0:T(8,128)S(1)}, u32[]{:S(2)}, u32[]{:S(2)}) %all-to-all-start.3) | async-done | bytes 524320 | tf_op jit(solution)/shard_map/all_to_all | solution.py:34
  179.7 0.6 broadcast_in_dim.27
  180.3 4.2 %all-to-all-start.5 = ((f32[32,1,256]{2,1,0:T(1,128)}), f32[32,1,256]{2,1,0:T(1,128)S(1)}, u32[]{:S(2)}, u32[]{:S(2)}) async-start(f32[32,1,256]{2,1,0:T(1,128)} %broadcast_in_dim.27), calls=%async_computation.5 | async-start | bytes 65536 | tf_op jit(solution)/shard_map/all_to_all | solution.py:34
  184.5 1.0 select_reduce_fusion.1
  186.0 11.7 %cholesky.206 = f32[128,128]{1,0:T(8,128)S(1)} custom-call(f32[128,128]{1,0:T(8,128)S(1)} %cholesky.273), custom_call_target="Cholesky" | custom-call | tf_op jit(solution)/shard_map/jit(cholesky)/cholesky | solution.py:20
  197.7 9.8 %custom-call.19 = f32[1,128,128]{1,2,0:T(8,128)S(1)} custom-call(f32[1,128,128]{2,1,0:T(8,128)S(1)} %get-tuple-element.67), custom_call_target="InvertDiagBlocksLowerTriangular" | custom-call | tf_op jit(solution)/shard_map/jit(cholesky)/cholesky | solution.py:20
  208.0 11.7 %cholesky.223 = f32[128,128]{1,0:T(8,128)S(1)} custom-call(f32[128,128]{1,0:T(8,128)S(1)} %convolution_subtract_fusion.7), custom_call_target="Cholesky" | custom-call | tf_op jit(solution)/shard_map/jit(cholesky)/cholesky | solution.py:20
  219.8 0.6 compare_reduce_fusion.2
  220.4 0.6 compare_reduce_fusion.3
  222.4 4.0 %while.7 = (s32[]{:T(128)}, f32[256,256]{1,0:T(8,128)S(1)}, s32[2,2]{1,0:T(2,128)S(1)}, f32[2,128,128]{2,1,0:T(8,128)S(1)}, s32[]{:T(128)}) while((s32[]{:T(128)}, f32[256,256]{1,0:T(8,128)S(1)}, s32[2,2]{1,0:T(2,128)S(1)}, f32[2,128,128]{2,1,0:T(8,128)S(1)}, s32[]{:T(128)}) %tuple.78), condition=%wide.while_cond.clone, body=%wide.while_body.clone.sunk | while | flops 2 | bytes 131181 | solution.py:21
  223.0 1.4 bitcast_dynamic-update-slice_fusion.7
  225.0 1.4 bitcast_dynamic-update-slice_fusion.7
  226.4 19.9 %custom-call.20 = f32[2,128,128]{1,2,0:T(8,128)S(1)} custom-call(f32[2,128,128]{2,1,0:T(8,128)S(1)} %get-tuple-element.26), custom_call_target="InvertDiagBlocksLowerTriangular" | custom-call | tf_op jit(solution)/shard_map/jit(_cho_solve)/triangular_solve | solution.py:21
  248.4 1.6 fusion
  250.1 24.7 %all_to_all.52 = f32[128,1,256]{2,1,0:T(1,128)S(1)} all-to-all(f32[128,1,256]{2,1,0:T(1,128)S(1)} %copy.58), channel_id=1, replica_groups=mesh['aa'=8,'y'=8,'core'=2,'col'=4] {'aa','y','core'}, dimensions={0} | all-to-all | bytes 262144 | tf_op jit(solution)/shard_map/all_to_all | solution.py:41
  274.8 0.8 broadcast_in_dim.28
  275.6 3.8 all-to-all-start.6
  279.5 17.2 %all-to-all-done.6 = f32[16,32,256]{2,1,0:T(8,128)S(1)} async-done(((f32[16,32,256]{2,1,0:T(8,128)}), f32[16,32,256]{2,1,0:T(8,128)S(1)}, u32[]{:S(2)}, u32[]{:S(2)}) %all-to-all-start.6) | async-done | bytes 524320 | tf_op jit(solution)/shard_map/all_to_all | solution.py:34
  296.7 1.0 select_reduce_fusion
  298.3 11.7 %cholesky.240 = f32[128,128]{1,0:T(8,128)S(1)} custom-call(f32[128,128]{1,0:T(8,128)S(1)} %cholesky.276), custom_call_target="Cholesky" | custom-call | tf_op jit(solution)/shard_map/jit(cholesky)/cholesky | solution.py:20
  310.0 9.8 %custom-call.21 = f32[1,128,128]{1,2,0:T(8,128)S(1)} custom-call(f32[1,128,128]{2,1,0:T(8,128)S(1)} %get-tuple-element.63), custom_call_target="InvertDiagBlocksLowerTriangular" | custom-call | tf_op jit(solution)/shard_map/jit(cholesky)/cholesky | solution.py:20
  320.3 11.7 %cholesky.257 = f32[128,128]{1,0:T(8,128)S(1)} custom-call(f32[128,128]{1,0:T(8,128)S(1)} %convolution_subtract_fusion.6), custom_call_target="Cholesky" | custom-call | tf_op jit(solution)/shard_map/jit(cholesky)/cholesky | solution.py:20
  332.1 0.6 compare_reduce_fusion
  332.7 0.6 compare_reduce_fusion.1
  334.7 4.0 %while.8 = (s32[]{:T(128)}, f32[256,256]{1,0:T(8,128)S(1)}, s32[2,2]{1,0:T(2,128)S(1)}, f32[2,128,128]{2,1,0:T(8,128)S(1)}, s32[]{:T(128)}) while((s32[]{:T(128)}, f32[256,256]{1,0:T(8,128)S(1)}, s32[2,2]{1,0:T(2,128)S(1)}, f32[2,128,128]{2,1,0:T(8,128)S(1)}, s32[]{:T(128)}) %tuple.79), condition=%wide.while_cond.clone.1, body=%wide.while_body.clone.1.sunk | while | flops 2 | bytes 131181 | solution.py:21
  335.3 1.4 bitcast_dynamic-update-slice_fusion.8
  336.7 0.6 fusion.106
  337.3 1.4 bitcast_dynamic-update-slice_fusion.8
  338.7 19.9 %custom-call.22 = f32[2,128,128]{1,2,0:T(8,128)S(1)} custom-call(f32[2,128,128]{2,1,0:T(8,128)S(1)} %get-tuple-element.27), custom_call_target="InvertDiagBlocksLowerTriangular" | custom-call | tf_op jit(solution)/shard_map/jit(_cho_solve)/triangular_solve | solution.py:21
  360.6 0.7 broadcast_in_dim.29
  361.3 5.9 %all-to-all-start.8 = ((f32[64,1,256]{2,1,0:T(1,128)}), f32[64,1,256]{2,1,0:T(1,128)S(1)}, u32[]{:S(2)}, u32[]{:S(2)}) async-start(f32[64,1,256]{2,1,0:T(1,128)} %broadcast_in_dim.29), calls=%async_computation.8 | async-start | bytes 131072 | tf_op jit(solution)/shard_map/all_to_all | solution.py:34
  367.8 8.7 %all-to-all-done.8 = f32[64,1,256]{2,1,0:T(1,128)S(1)} async-done(((f32[64,1,256]{2,1,0:T(1,128)}), f32[64,1,256]{2,1,0:T(1,128)S(1)}, u32[]{:S(2)}, u32[]{:S(2)}) %all-to-all-start.8) | async-done | bytes 65568 | tf_op jit(solution)/shard_map/all_to_all | solution.py:34
  376.6 0.6 broadcast_in_dim.30
  377.2 3.3 all-to-all-start.9
  381.1 5.9 %all-to-all-done.9 = f32[8,1,256]{2,1,0:T(1,128)S(1)} async-done(((f32[8,1,256]{2,1,0:T(1,128)}), f32[8,1,256]{2,1,0:T(1,128)S(1)}, u32[]{:S(2)}, u32[]{:S(2)}) %all-to-all-start.9) | async-done | bytes 8224 | tf_op jit(solution)/shard_map/all_to_all | solution.py:34
  (102 shorter events, 14.8 us)
Async XLA Ops:
  0.6 113.1 %copy-start = (bf16[64,32,128]{2,1,0:T(8,128)(2,1)S(1)}, bf16[64,32,128]{2,1,0:T(8,128)(2,1)}, u32[]{:S(2)}) copy-start(bf16[64,32,128]{2,1,0:T(8,128)(2,1)} %param.6) | copy-start | bytes 1572868
  42.3 6.6 %collective-permute-start = (f32[256,512]{1,0:T(8,128)S(1)}, f32[256,512]{1,0:T(8,128)S(1)}, u32[]{:S(2)}, u32[]{:S(2)}) collective-permute-start(f32[256,512]{1,0:T(8,128)S(1)} %bitcast.167), channel_id=1, source_target_pairs={{0,4},{4,0},{1,5},{5,1},{2,6},{6,2},{3,7},{7,3},{8,12},{12,8},{9,1... | collective-permute-start | bytes 1572872 | tf_op jit(solution)/shard_map/ppermute | solution.py:58
  111.2 1.3 copy-start.4
  111.5 0.7 copy-start.1
  115.8 14.9 %all-to-all-start.1 = ((f32[64,1,256]{2,1,0:T(1,128)}), f32[64,1,256]{2,1,0:T(1,128)}, u32[]{:S(2)}, u32[]{:S(2)}) async-start(f32[64,1,256]{2,1,0:T(1,128)} %reshape.121), calls=%async_computation.1 | async-start | bytes 131072 | tf_op jit(solution)/shard_map/all_to_all | solution.py:41
  132.3 14.7 %all-to-all-start.2 = ((f32[64,1,256]{2,1,0:T(1,128)}), f32[64,1,256]{2,1,0:T(1,128)S(1)}, u32[]{:S(2)}, u32[]{:S(2)}) async-start(f32[64,1,256]{2,1,0:T(1,128)} %broadcast_in_dim.24), calls=%async_computation.2 | async-start | bytes 131072 | tf_op jit(solution)/shard_map/all_to_all | solution.py:34
  147.2 14.0 %copy-start.2 = (f32[64,256]{1,0:T(8,128)}, f32[64,256]{1,0:T(8,128)S(1)}, u32[]{:S(2)}) copy-start(f32[64,256]{1,0:T(8,128)S(1)} %fusion.9) | copy-start | bytes 196612
  161.2 18.5 %all-to-all-start.3 = ((f32[8,64,256]{2,1,0:T(8,128)}), f32[8,64,256]{2,1,0:T(8,128)S(1)}, u32[]{:S(2)}, u32[]{:S(2)}) async-start(f32[8,64,256]{2,1,0:T(8,128)} %broadcast_in_dim.25), calls=%async_computation.3 | async-start | bytes 1048576 | tf_op jit(solution)/shard_map/all_to_all | solution.py:34
  180.3 67.8 %all-to-all-start.5 = ((f32[32,1,256]{2,1,0:T(1,128)}), f32[32,1,256]{2,1,0:T(1,128)S(1)}, u32[]{:S(2)}, u32[]{:S(2)}) async-start(f32[32,1,256]{2,1,0:T(1,128)} %broadcast_in_dim.27), calls=%async_computation.5 | async-start | bytes 65536 | tf_op jit(solution)/shard_map/all_to_all | solution.py:34
  207.8 40.3 %copy-start.3 = (f32[64,256]{1,0:T(8,128)S(1)}, f32[64,256]{1,0:T(8,128)}, u32[]{:S(2)}) copy-start(f32[64,256]{1,0:T(8,128)} %copy-done.2) | copy-start | bytes 196612
  275.6 21.1 %all-to-all-start.6 = ((f32[16,32,256]{2,1,0:T(8,128)}), f32[16,32,256]{2,1,0:T(8,128)S(1)}, u32[]{:S(2)}, u32[]{:S(2)}) async-start(f32[16,32,256]{2,1,0:T(8,128)} %broadcast_in_dim.28), calls=%async_computation.6 | async-start | bytes 1048576 | tf_op jit(solution)/shard_map/all_to_all | solution.py:34
  361.3 15.2 %all-to-all-start.8 = ((f32[64,1,256]{2,1,0:T(1,128)}), f32[64,1,256]{2,1,0:T(1,128)S(1)}, u32[]{:S(2)}, u32[]{:S(2)}) async-start(f32[64,1,256]{2,1,0:T(1,128)} %broadcast_in_dim.29), calls=%async_computation.8 | async-start | bytes 131072 | tf_op jit(solution)/shard_map/all_to_all | solution.py:34
  377.2 9.9 %all-to-all-start.9 = ((f32[8,1,256]{2,1,0:T(1,128)}), f32[8,1,256]{2,1,0:T(1,128)S(1)}, u32[]{:S(2)}, u32[]{:S(2)}) async-start(f32[8,1,256]{2,1,0:T(1,128)} %broadcast_in_dim.30), calls=%async_computation.9 | async-start | bytes 16384 | tf_op jit(solution)/shard_map/all_to_all | solution.py:34
